TPU v7x, 32 devices: a whole 2x2x4 slice. The times are simulated.
32 devices in a mesh: groups: 2 (over y), layer: 4 (over z), dp: 2 (over x), chan: 2 (over core).
Axes of the slice: x: 2, y: 2, z: 4, core: 2. Of those that a mesh axis runs over, the one named last changes fastest.
Arguments:
- activations: bfloat16 [4, 4, 32, 16, 16, 128], P('layer', None, ('groups', 'dp', 'chan')), parts along dimension 2, may hold values from -0.94921875 to 0.94921875
- weights: bfloat16 [4, 4, 9, 128, 128], P('layer'), may hold values from -0.1875 to 0.1875
- guesses: bfloat16 [4, 32, 16, 16, 128], P('layer', ('groups', 'dp', 'chan')), parts along dimension 1, may hold values from -6 to 6
- terminal: bfloat16 [32, 16, 16, 128], P(('groups', 'dp', 'chan')), parts along dimension 0, may hold values from -6 to 6
- coarse_rates: float32 [4, 128], P('layer'), may hold values from 0.0074 to 1, as said below
- block_layers: int32 [4], P('layer'), may hold values from 1 to 4, 12 in all
Outputs:
- corrected: bfloat16 [4, 32, 16, 16, 128], P('layer', ('groups', 'dp', 'chan')), parts along dimension 1
- kernel_grads: bfloat16 [8, 4, 9, 128, 128], P(('groups', 'layer')), parts along dimension 0
There are 2 independent parts, one for each index of `groups`. A program takes and returns all parts, laid end to end along the dimension named above; an argument that names none is the same for every part. Nothing has to cross between parts.
Inputs may be any that keep to these rules, and one draw needn't show every extreme that they name: `block_layers`: every block holds at least one layer and some block holds exactly 4; the counts sum to 12. `coarse_rates`: strictly positive.
All inputs are finite; a program needn't handle non-finite values.
Results may differ from a plain program's by a relative error of at most 0.0055.
Values may be sent and summed in bfloat16 or wider, within the bound.
A program may use at most 64 MiB of HBM per device.

v0:
```python
import jax
import jax.numpy as jnp
from jax import lax
from jax.sharding import PartitionSpec as P

MMAX = 4
step_size = 0.25
OFFSETS = [(row_off, col_off) for row_off in (-1, 0, 1) for col_off in (-1, 0, 1)]


def shifted(value, axis, steps):
    count = lax.axis_size(axis)
    first, last = (max(0, -steps), min(count, count - steps))
    return lax.ppermute(value, axis, [(source, source + steps) for source in range(first, last)])


def entering(part, axis, combine, identity):
    count = lax.axis_size(axis)
    place = lax.axis_index(axis)
    ahead = count - 1 - place
    gathered = jax.tree.map(lambda a: lax.all_gather(a, axis), part)
    state = jax.tree.map(lambda a, e: jnp.zeros_like(a) + jnp.asarray(e, a.dtype), part, identity)

    def one(turn, state):
        source = count - 1 - turn
        return combine(
            state, jax.tree.map(lambda a: lax.dynamic_index_in_dim(a, source, 0, False), gathered)
        )

    return lax.fori_loop(0, ahead, one, state)


def adjoint_step(adjoint, activation, kernel):
    map_side = adjoint.shape[1]
    rounded = adjoint.astype(jnp.bfloat16)
    padded = jnp.pad(rounded, ((0, 0), (1, 1), (1, 1), (0, 0)))
    summed = jnp.zeros(adjoint.shape, jnp.float32)
    for index, (row_off, col_off) in enumerate(OFFSETS):
        sliced = padded[
            :, 1 - row_off : 1 - row_off + map_side, 1 - col_off : 1 - col_off + map_side, :
        ]
        summed = summed + jnp.dot(sliced, kernel[index].T, preferred_element_type=jnp.float32)
    act_float = activation.astype(jnp.float32)
    return (adjoint + step_size * (1.0 - act_float * act_float) * summed, rounded)


def kernel_grad(activation, rounded):
    map_side = rounded.shape[1]
    padded = jnp.pad(activation, ((0, 0), (1, 1), (1, 1), (0, 0)))
    pieces = []
    for row_off, col_off in OFFSETS:
        sliced = padded[
            :, 1 + row_off : 1 + row_off + map_side, 1 + col_off : 1 + col_off + map_side, :
        ]
        pieces.append(
            lax.dot_general(
                sliced,
                rounded,
                (((0, 1, 2), (0, 1, 2)), ((), ())),
                preferred_element_type=jnp.float32,
            )
        )
    return step_size * jnp.stack(pieces)


def per_device(activations, weights, guesses, terminal, coarse_rates, block_layers):
    layer_count = block_layers[0]
    acts_block = activations[0]
    kernels_block = weights[0]
    at_end = lax.axis_index("layer") == lax.axis_size("layer") - 1
    end_state = terminal.astype(jnp.float32)
    own_guess = guesses[0].astype(jnp.float32)
    received = shifted(guesses, "layer", -1)[0]
    adjoint = jnp.where(at_end, end_state, received.astype(jnp.float32))
    for slot in reversed(range(MMAX)):
        stepped, _ = adjoint_step(adjoint, acts_block[slot], kernels_block[slot])
        adjoint = jnp.where(slot < layer_count, stepped, adjoint)
    residual = adjoint - own_guess
    rates = coarse_rates[0]

    def compose(earlier, later):
        return (later[0] * earlier[0], later[1] + later[0] * earlier[1])

    identity = (jnp.ones_like(rates), jnp.zeros_like(residual))
    _, following = entering((rates, residual), "layer", compose, identity)
    correction = residual + rates * following
    corrected = (own_guess + correction).astype(jnp.bfloat16)
    received = shifted(corrected[None], "layer", -1)[0]
    adjoint = jnp.where(at_end, end_state, received.astype(jnp.float32))
    slot_list = [None] * MMAX
    for slot in reversed(range(MMAX)):
        stepped, rounded = adjoint_step(adjoint, acts_block[slot], kernels_block[slot])
        active = slot < layer_count
        slot_grad = kernel_grad(acts_block[slot], rounded)
        slot_grad = jnp.where(active, slot_grad, jnp.zeros_like(slot_grad))
        slot_list[slot] = slot_grad
        adjoint = jnp.where(active, stepped, adjoint)
    stacked = jnp.stack(slot_list)
    result = lax.psum(stacked, ("dp", "chan")).astype(jnp.bfloat16)
    return (corrected[None], result[None])


def solution(mesh):
    in_specs = (
        P("layer", None, ("groups", "dp", "chan"), None, None, None),
        P("layer", None, None, None, None),
        P("layer", ("groups", "dp", "chan"), None, None, None),
        P(("groups", "dp", "chan"), None, None, None),
        P("layer", None),
        P("layer"),
    )
    out_specs = (
        P("layer", ("groups", "dp", "chan"), None, None, None),
        P(("groups", "layer"), None, None, None, None),
    )
    return jax.shard_map(
        per_device, mesh=mesh, in_specs=in_specs, out_specs=out_specs, check_vma=False
    )
```

profile of v0, /device:TPU:0, one launch (start us, length us, event | category | flops | bytes accessed | tf_op | source)
XLA Modules:
  0.0 162.6 jit_solution(5716062791998601039)
XLA Ops:
  7.2 1.4 collective-permute-start
  9.3 9.5 %collective-permute-done = bf16[1,4,16,16,128]{4,3,2,1,0:T(8,128)(2,1)S(1)} collective-permute-done((bf16[1,4,16,16,128]{4,3,2,1,0:T(8,128)(2,1)}, bf16[1,4,16,16,128]{4,3,2,1,0:T(8,128)(2,1)S(1)}, u32[]{:S(2)}, u32[]{:S(2)}) %collective-permute-start) | collective-permute-done | bytes 262176 | tf_op jit(solution)/shard_map/ppermute | solution.py:14
  18.8 1.0 fusion.60
  19.8 1.0 fusion.63
  21.8 0.2 convolution_add_fusion.51
  22.5 0.7 copy-done
  23.3 0.3 fusion.284
  25.0 0.2 convolution_add_fusion.42
  25.5 0.3 fusion.285
  27.7 0.3 fusion.286
  29.9 0.5 copy-done.4
  30.4 1.1 fusion.12
  31.5 9.3 %all-gather.1 = f32[4,1,128]{2,1,0:T(1,128)S(1)} all-gather(f32[1,1,128]{2,1,0:T(1,128)S(1)} %bitcast.708), channel_id=1, replica_groups=mesh['groups'=2,'layer'=4,'dp'=2,'chan'=2] {'layer'}, dimensions={0}, use_global_device_ids=true | all-gather | bytes 2560 | tf_op jit(solution)/shard_map/all_gather | solution.py:21
  40.9 37.1 %all-gather.4.cloned.1.call-done = f32[16,16,16,128]{3,2,1,0:T(8,128)} async-done(((f32[4,16,16,128]{3,2,1,0:T(8,128)}), f32[16,16,16,128]{3,2,1,0:T(8,128)}) %all-gather.4.cloned.1.call-update) | async-done | bytes 2097168 | tf_op jit(solution)/shard_map/all_gather | solution.py:21
  78.0 3.9 %while.14 = (s32[]{:T(128)}, f32[4,16,16,128]{3,2,1,0:T(8,128)S(1)}, s32[]{:T(128)}, f32[4,4,16,16,128]{4,3,2,1,0:T(8,128)}, f32[4,128]{1,0:T(4,128)S(1)}, /*index=5*/s32[]{:T(128)}, s32[]{:T(128)}, s32[]{:T(128)}, s32[]{:T(128)}) while((s32[]{:T(128)}, f32[4,16,16,128]{3,2,1,0:T(8,128)S(1)}, s32[]{:T(128)}, f32[4,4,16,16,128]{4,3,2,1,0:T(8,128)}, ...), condition=%wide.region_1.2_spmd, body=%wide.region_0.1_spmd.sunk | while | flops 262150 | bytes 1574555 | solution.py:30
  78.1 1.3 bitcast_add_fusion.2
  79.4 1.2 bitcast_add_fusion.2
  80.7 1.2 bitcast_add_fusion.2
  82.0 1.0 fusion.62
  83.0 1.5 collective-permute-start.1
  84.7 8.3 %collective-permute-done.1 = bf16[1,4,16,16,128]{4,3,2,1,0:T(8,128)(2,1)S(1)} collective-permute-done((bf16[1,4,16,16,128]{4,3,2,1,0:T(8,128)(2,1)S(1)}, bf16[1,4,16,16,128]{4,3,2,1,0:T(8,128)(2,1)S(1)}, u32[]{:S(2)}, u32[]{:S(2)}) %collective-permute-start.1) | collective-permute-done | bytes 262176 | tf_op jit(solution)/shard_map/ppermute | solution.py:14
  94.2 0.2 convolution_add_fusion.19
  94.9 0.3 fusion.287
  95.5 0.2 convolution_add_fusion.15
  97.2 0.3 fusion.288
  99.4 0.3 fusion.22
  99.7 0.3 fusion.58
  99.9 0.3 fusion.57
  100.2 0.3 fusion.56
  100.5 0.3 fusion.55
  100.8 0.3 fusion.54
  101.1 0.3 fusion.53
  101.3 0.3 fusion.52
  101.6 0.3 fusion.51
  101.9 0.3 fusion.50
  102.2 0.3 fusion.40
  102.5 0.3 fusion.39
  102.8 0.3 fusion.38
  103.0 0.3 fusion.37
  103.3 0.3 fusion.36
  103.6 0.3 fusion.35
  103.9 0.3 fusion.34
  104.2 0.3 fusion.33
  104.4 0.3 fusion.32
  104.7 0.3 fusion.31
  105.0 0.3 fusion.30
  105.3 0.3 fusion.29
  105.6 0.3 fusion.28
  105.8 0.3 fusion.27
  106.1 0.3 fusion.26
  106.4 0.3 fusion.25
  106.7 0.3 fusion.24
  107.0 0.3 fusion.23
  107.3 0.3 fusion.49
  107.5 0.3 fusion.48
  107.8 0.3 fusion.47
  108.1 0.3 fusion.46
  108.4 0.3 fusion.45
  108.7 0.3 fusion.44
  108.9 0.3 fusion.43
  109.2 0.3 fusion.42
  109.5 0.3 fusion.41
  110.0 0.2 pad_maximum_fusion
  110.3 45.5 %all-reduce.12 = bf16[4,9,128,128]{3,2,1,0:T(8,128)(2,1)} all-reduce(f32[4,9,128,128]{3,2,1,0:T(8,128)S(1)} %pad_maximum_fusion), channel_id=1, replica_groups=mesh['groups'=2,'layer'=4,'dp'=2,'chan'=2] {'dp','chan'}, use_global_device_ids=true, to_apply=%region_2.3 | all-reduce | flops 589824 | bytes 3538944 | tf_op jit(solution)/shard_map/psum | solution.py:99
  (73 shorter events, 12.4 us)
Async XLA Ops:
  7.2 13.7 %copy-start.3 = (bf16[1,4,9,128,128]{4,3,2,1,0:T(8,128)(2,1)S(1)}, bf16[1,4,9,128,128]{4,3,2,1,0:T(8,128)(2,1)}, u32[]{:S(2)}) copy-start(bf16[1,4,9,128,128]{4,3,2,1,0:T(8,128)(2,1)} %param.9) | copy-start | bytes 3538948
  7.2 70.8 %all-gather.4.cloned.1.call-start = ((), (), s32[]{:S(2)}) async-start(), calls=%async_computation | async-start | bytes 2621440 | tf_op jit(solution)/shard_map/all_gather | solution.py:21
  7.2 11.6 %collective-permute-start = (bf16[1,4,16,16,128]{4,3,2,1,0:T(8,128)(2,1)}, bf16[1,4,16,16,128]{4,3,2,1,0:T(8,128)(2,1)S(1)}, u32[]{:S(2)}, u32[]{:S(2)}) collective-permute-start(bf16[1,4,16,16,128]{4,3,2,1,0:T(8,128)(2,1)} %param.10), channel_id=1, source_target_pairs={{4,0},{8,4},{12,8},{5,1},{9,5},{13,9},{6,2},{10,6},{14,10},{7,3},{... | collective-permute-start | bytes 786440 | tf_op jit(solution)/shard_map/ppermute | solution.py:14
  22.0 1.2 copy-start
  22.0 1.3 copy-start.2
  29.4 1.0 copy-start.4
  30.4 1.1 copy-start.6
  78.0 3.9 %copy-start.1 = (f32[4,16,16,128]{3,2,1,0:T(8,128)S(1)}, f32[4,16,16,128]{3,2,1,0:T(8,128)}, u32[]{:S(2)}) copy-start(f32[4,16,16,128]{3,2,1,0:T(8,128)} %fusion.12) | copy-start | bytes 1572868
  83.0 10.0 %copy-start.5 = (bf16[1,4,16,16,128]{4,3,2,1,0:T(8,128)(2,1)}, bf16[1,4,16,16,128]{4,3,2,1,0:T(8,128)(2,1)S(1)}, u32[]{:S(2)}) copy-start(bf16[1,4,16,16,128]{4,3,2,1,0:T(8,128)(2,1)S(1)} %fusion.62) | copy-start | bytes 786436
  83.0 9.9 %collective-permute-start.1 = (bf16[1,4,16,16,128]{4,3,2,1,0:T(8,128)(2,1)S(1)}, bf16[1,4,16,16,128]{4,3,2,1,0:T(8,128)(2,1)S(1)}, u32[]{:S(2)}, u32[]{:S(2)}) collective-permute-start(bf16[1,4,16,16,128]{4,3,2,1,0:T(8,128)(2,1)S(1)} %fusion.62), channel_id=1, source_target_pairs={{4,0},{8,4},{12,8},{5,1},{9,5},{13,9},{6,2},{10,6},{14,10},{7,3},{... | collective-permute-start | bytes 786440 | tf_op jit(solution)/shard_map/ppermute | solution.py:14
Sparse Core Ops, SparseCore 0:
  31.6 46.3 all-gather.3
where the time goes:
time: 163 us
  waiting for transfers between devices  54.9 us (34%)
  blocking collectives  54.8 us (34%)
  matrix products  26.5 us (16%)
  between operations  15.5 us (10%)
  other arithmetic  6.39 us (4%)
  starting transfers between devices  2.93 us (2%)
    psum x1, blocking collectives, per_device(): result = lax.psum(stacked, ('dp', 'chan')).astype(jnp.bfloat16)  45.5 us
    all_gather x1, waiting for transfers between devices, entering(): gathered = jax.tree.map(lambda a: lax.all_gather(a, axis), part)  37.1 us
    ppermute x2, waiting for transfers between devices, shifted(): lax.ppermute(value, axis, [(source, source + steps) for source in range(f...  17.7 us
    dot_general x63, matrix products, adjoint_step(): jnp.dot(sliced, kernel[index].T, preferred_element_type=jnp.float32)  16.6 us
    dot_general x36, matrix products, kernel_grad(): lax.dot_general(sliced, rounded, (((0, 1, 2), (0, 1, 2)), ((), ())), pref...  9.87 us
    all_gather x1, blocking collectives, entering(): gathered = jax.tree.map(lambda a: lax.all_gather(a, axis), part)  9.34 us
    add x3, other arithmetic, compose(): return (later[0] * earlier[0], later[1] + later[0] * earlier[1])  3.78 us
  transfers between devices with their start and end apart: 3, of which 3 were waited for; matrix products, arithmetic and copies ran while one was open for 0% of the time, Pallas kernels for 0%

commit v1 on v0

--- a/solution.py
+++ b/solution.py
@@ -6,6 +6,9 @@
 MMAX = 4
 step_size = 0.25
 OFFSETS = [(row_off, col_off) for row_off in (-1, 0, 1) for col_off in (-1, 0, 1)]
+group_roots_on_mesh = lambda block_in: lax.all_gather(block_in, axis_name=("dp", "chan")).sum(
+    axis=0
+)
 
 
 def shifted(value, axis, steps):
@@ -96,7 +99,7 @@
         slot_list[slot] = slot_grad
         adjoint = jnp.where(active, stepped, adjoint)
     stacked = jnp.stack(slot_list)
-    result = lax.psum(stacked, ("dp", "chan")).astype(jnp.bfloat16)
+    result = group_roots_on_mesh(stacked).astype(jnp.bfloat16)
     return (corrected[None], result[None])
 
 

time: 163 us -> 188 us (1.15)
  waiting for transfers between devices: 54.9 us -> 117 us
  blocking collectives: 54.8 us -> 9.34 us
  other arithmetic: 6.39 us -> 13.8 us
    all_gather x0 -> x1, waiting for transfers between devices: none -> 62.5 us  [lax.all_gather(block_in, axis_name=('dp', 'chan')).sum(axis=0)]
    psum x1 -> x0, blocking collectives: 45.5 us -> none  [per_device(): result = lax.psum(stacked, ('dp', 'chan')).astype(jnp.bfloat16)]
    reduce_sum x0 -> x1, other arithmetic: none -> 6.03 us  [lax.all_gather(block_in, axis_name=('dp', 'chan')).sum(axis=0)]
  transfers between devices with their start and end apart: 3 -> 4, of which waited for: 3 -> 4; matrix products, arithmetic and copies ran while one was open for 0% -> 0% of each run, Pallas kernels for 0% -> 0%
where the time goes in v1:
time: 188 us; the launch traced here: 187 us
  waiting for transfers between devices  117 us (62%)
  matrix products  26.4 us (14%)
  between operations  15.5 us (8%)
  other arithmetic  13.8 us (7%)
  blocking collectives  9.34 us (5%)
  starting transfers between devices  2.98 us (2%)
    all_gather x1, waiting for transfers between devices, lax.all_gather(block_in, axis_name=('dp', 'chan')).sum(axis=0)  62.5 us
    all_gather x1, waiting for transfers between devices, entering(): gathered = jax.tree.map(lambda a: lax.all_gather(a, axis), part)  37.1 us
    ppermute x2, waiting for transfers between devices, shifted(): lax.ppermute(value, axis, [(source, source + steps) for source in range(f...  17.7 us
    dot_general x63, matrix products, adjoint_step(): jnp.dot(sliced, kernel[index].T, preferred_element_type=jnp.float32)  16.6 us
    dot_general x36, matrix products, kernel_grad(): lax.dot_general(sliced, rounded, (((0, 1, 2), (0, 1, 2)), ((), ())), pref...  9.81 us
    all_gather x1, blocking collectives, entering(): gathered = jax.tree.map(lambda a: lax.all_gather(a, axis), part)  9.34 us
    reduce_sum x1, other arithmetic, lax.all_gather(block_in, axis_name=('dp', 'chan')).sum(axis=0)  6.03 us
    add x3, other arithmetic, compose(): return (later[0] * earlier[0], later[1] + later[0] * earlier[1])  3.78 us
  transfers between devices with their start and end apart: 4, of which 4 were waited for; matrix products, arithmetic and copies ran while one was open for 0% of the time, Pallas kernels for 0%

profile of v1, /device:TPU:0, one launch (start us, length us, event | category | flops | bytes accessed | tf_op | source)
XLA Modules:
  0.0 187.0 jit_solution(14316713710736795717)
XLA Ops:
  7.2 1.4 collective-permute-start
  9.3 9.5 %collective-permute-done = bf16[1,4,16,16,128]{4,3,2,1,0:T(8,128)(2,1)S(1)} collective-permute-done((bf16[1,4,16,16,128]{4,3,2,1,0:T(8,128)(2,1)}, bf16[1,4,16,16,128]{4,3,2,1,0:T(8,128)(2,1)S(1)}, u32[]{:S(2)}, u32[]{:S(2)}) %collective-permute-start) | collective-permute-done | bytes 262176 | tf_op jit(solution)/shard_map/ppermute | solution.py:17
  18.8 1.0 fusion.60
  19.8 1.0 fusion.63
  21.8 0.2 convolution_add_fusion.51
  22.5 0.7 copy-done
  23.3 0.3 fusion.284
  25.5 0.3 fusion.285
  26.0 0.2 convolution_add_fusion.39
  27.7 0.3 fusion.286
  29.9 0.5 copy-done.4
  30.4 1.1 fusion.12
  31.6 9.3 %all-gather.2 = f32[4,1,128]{2,1,0:T(1,128)S(1)} all-gather(f32[1,1,128]{2,1,0:T(1,128)S(1)} %bitcast.710), channel_id=1, replica_groups=mesh['groups'=2,'layer'=4,'dp'=2,'chan'=2] {'layer'}, dimensions={0}, use_global_device_ids=true | all-gather | bytes 2560 | tf_op jit(solution)/shard_map/all_gather | solution.py:24
  40.9 37.1 %all-gather.6.cloned.1.call-done = f32[16,16,16,128]{3,2,1,0:T(8,128)} async-done(((f32[4,16,16,128]{3,2,1,0:T(8,128)}), f32[16,16,16,128]{3,2,1,0:T(8,128)}) %all-gather.6.cloned.1.call-update) | async-done | bytes 2097168 | tf_op jit(solution)/shard_map/all_gather | solution.py:24
  78.0 3.9 %while.14 = (s32[]{:T(128)}, f32[4,16,16,128]{3,2,1,0:T(8,128)S(1)}, s32[]{:T(128)}, f32[4,4,16,16,128]{4,3,2,1,0:T(8,128)}, f32[4,128]{1,0:T(4,128)S(1)}, /*index=5*/s32[]{:T(128)}, s32[]{:T(128)}, s32[]{:T(128)}, s32[]{:T(128)}) while((s32[]{:T(128)}, f32[4,16,16,128]{3,2,1,0:T(8,128)S(1)}, s32[]{:T(128)}, f32[4,4,16,16,128]{4,3,2,1,0:T(8,128)}, ...), condition=%wide.region_1.2_spmd, body=%wide.region_0.1_spmd.sunk | while | flops 262150 | bytes 1574555 | solution.py:33
  78.1 1.3 bitcast_add_fusion.2
  79.4 1.2 bitcast_add_fusion.2
  80.7 1.2 bitcast_add_fusion.2
  82.0 1.0 fusion.62
  83.0 1.5 collective-permute-start.1
  84.7 8.3 %collective-permute-done.1 = bf16[1,4,16,16,128]{4,3,2,1,0:T(8,128)(2,1)S(1)} collective-permute-done((bf16[1,4,16,16,128]{4,3,2,1,0:T(8,128)(2,1)S(1)}, bf16[1,4,16,16,128]{4,3,2,1,0:T(8,128)(2,1)S(1)}, u32[]{:S(2)}, u32[]{:S(2)}) %collective-permute-start.1) | collective-permute-done | bytes 262176 | tf_op jit(solution)/shard_map/ppermute | solution.py:17
  94.9 0.3 fusion.287
  97.2 0.3 fusion.288
  97.7 0.2 convolution_add_fusion.7
  99.4 0.3 fusion.22
  99.7 0.3 fusion.58
  99.9 0.3 fusion.57
  100.2 0.3 fusion.56
  100.5 0.3 fusion.55
  100.8 0.3 fusion.54
  101.0 0.3 fusion.53
  101.3 0.3 fusion.52
  101.6 0.3 fusion.51
  101.9 0.3 fusion.50
  102.2 0.3 fusion.40
  102.4 0.3 fusion.39
  102.7 0.3 fusion.38
  103.0 0.3 fusion.37
  103.3 0.3 fusion.36
  103.6 0.3 fusion.35
  103.8 0.3 fusion.34
  104.1 0.3 fusion.33
  104.4 0.3 fusion.32
  104.7 0.3 fusion.31
  105.0 0.3 fusion.30
  105.2 0.3 fusion.29
  105.5 0.3 fusion.28
  105.8 0.3 fusion.27
  106.1 0.3 fusion.26
  106.4 0.3 fusion.25
  106.6 0.3 fusion.24
  106.9 0.3 fusion.23
  107.2 0.3 fusion.49
  107.5 0.3 fusion.48
  107.8 0.3 fusion.47
  108.0 0.3 fusion.46
  108.3 0.3 fusion.45
  108.6 0.3 fusion.44
  108.9 0.3 fusion.43
  109.2 0.3 fusion.42
  109.4 0.3 fusion.41
  110.0 1.6 pad_maximum_fusion
  111.6 62.5 %all-gather.8.cloned.1.call-done = f32[16,9,128,128]{3,2,1,0:T(8,128)} async-done(((f32[4,9,128,128]{3,2,1,0:T(8,128)}), f32[16,9,128,128]{3,2,1,0:T(8,128)}) %all-gather.8.cloned.1.call-update) | async-done | bytes 9437200 | tf_op jit(solution)/shard_map/all_gather | solution.py:9
  174.1 6.0 %reduce_sum.9 = bf16[4,9,128,128]{3,2,1,0:T(8,128)(2,1)} reduce(f32[4,4,9,128,128]{4,3,2,1,0:T(8,128)} %bitcast.707, f32[]{:T(128)} %constant.62.clone.1), dimensions={0}, to_apply=%region_2.3 | reduce | flops 1769472 | bytes 10616836 | tf_op jit(solution)/shard_map/reduce_sum | solution.py:9
  (76 shorter events, 12.8 us)
Async XLA Ops:
  7.2 13.7 %copy-start.3 = (bf16[1,4,9,128,128]{4,3,2,1,0:T(8,128)(2,1)S(1)}, bf16[1,4,9,128,128]{4,3,2,1,0:T(8,128)(2,1)}, u32[]{:S(2)}) copy-start(bf16[1,4,9,128,128]{4,3,2,1,0:T(8,128)(2,1)} %param.9) | copy-start | bytes 3538948
  7.2 70.8 %all-gather.6.cloned.1.call-start = ((), (), s32[]{:S(2)}) async-start(), calls=%async_computation | async-start | bytes 2621440 | tf_op jit(solution)/shard_map/all_gather | solution.py:24
  7.2 11.6 %collective-permute-start = (bf16[1,4,16,16,128]{4,3,2,1,0:T(8,128)(2,1)}, bf16[1,4,16,16,128]{4,3,2,1,0:T(8,128)(2,1)S(1)}, u32[]{:S(2)}, u32[]{:S(2)}) collective-permute-start(bf16[1,4,16,16,128]{4,3,2,1,0:T(8,128)(2,1)} %param.10), channel_id=1, source_target_pairs={{4,0},{8,4},{12,8},{5,1},{9,5},{13,9},{6,2},{10,6},{14,10},{7,3},{... | collective-permute-start | bytes 786440 | tf_op jit(solution)/shard_map/ppermute | solution.py:17
  22.0 1.2 copy-start
  22.0 1.3 copy-start.2
  29.4 1.0 copy-start.4
  30.4 1.2 copy-start.6
  31.5 142.6 %all-gather.8.cloned.1.call-start = ((), (), s32[]{:S(2)}) async-start(), calls=%async_computation.1 | async-start | bytes 11796480 | tf_op jit(solution)/shard_map/all_gather | solution.py:9
  78.0 3.9 %copy-start.1 = (f32[4,16,16,128]{3,2,1,0:T(8,128)S(1)}, f32[4,16,16,128]{3,2,1,0:T(8,128)}, u32[]{:S(2)}) copy-start(f32[4,16,16,128]{3,2,1,0:T(8,128)} %fusion.12) | copy-start | bytes 1572868
  83.0 10.0 %copy-start.5 = (bf16[1,4,16,16,128]{4,3,2,1,0:T(8,128)(2,1)}, bf16[1,4,16,16,128]{4,3,2,1,0:T(8,128)(2,1)S(1)}, u32[]{:S(2)}) copy-start(bf16[1,4,16,16,128]{4,3,2,1,0:T(8,128)(2,1)S(1)} %fusion.62) | copy-start | bytes 786436
  83.0 9.9 %collective-permute-start.1 = (bf16[1,4,16,16,128]{4,3,2,1,0:T(8,128)(2,1)S(1)}, bf16[1,4,16,16,128]{4,3,2,1,0:T(8,128)(2,1)S(1)}, u32[]{:S(2)}, u32[]{:S(2)}) collective-permute-start(bf16[1,4,16,16,128]{4,3,2,1,0:T(8,128)(2,1)S(1)} %fusion.62), channel_id=1, source_target_pairs={{4,0},{8,4},{12,8},{5,1},{9,5},{13,9},{6,2},{10,6},{14,10},{7,3},{... | collective-permute-start | bytes 786440 | tf_op jit(solution)/shard_map/ppermute | solution.py:17
Sparse Core Ops, SparseCore 0:
  31.6 46.3 all-gather.5
  111.8 62.3 all-gather.7
